TPU v7x, 256 devices: a whole 4x4x8 slice. The times are simulated.
256 devices in a mesh: sub: 4 (over y_hi, core), row: 8 (over z), col: 8 (over y_lo, x).
Axes of the slice: x: 4, y: 4 (y_hi: 2, y_lo: 2; y = y_hi * 2 + y_lo), z: 8, core: 2. Of those that a mesh axis runs over, the one named last changes fastest.
Arguments:
- front: float32 [8192, 8192], P('row', ('sub', 'col')), may hold values from -3072 to 5120, as said below
- children: float32 [8, 2048, 8192], P('sub', 'row', 'col'), may hold values from -1 to 1, as said below
- child_map: int32 [8, 16], replicated, may hold values from 0 to 63, as said below
Outputs:
- factored: float32 [8192, 8192], P('row', ('sub', 'col'))
Inputs may be any that keep to these rules, and one draw needn't show every extreme that they name: For each child k the entries child_map[k, b] are distinct, and child_map[k, b] % 8 == b // 2. The entries of front in the rows and columns of front blocks below 8, in front order, form a symmetric matrix whose smallest eigenvalue is at least 1024. Entries of children in columns that stand for front column blocks below 8 lie within -0.0625 to 0.0625.
All inputs are finite; a program needn't handle non-finite values.
Results may differ from a plain program's by a relative error of at most 0.00009.
Values sent between devices are 32-bit elements; how exact they have to be, the bound alone decides.
No kernel may reach another device: no remote copies, remote signals or barrier semaphores. Data moves between devices by JAX's collectives and lax.ppermute only.
A program may use at most 128 MiB of HBM per device.

v0:
```python
import jax
import jax.numpy as jnp
from jax import lax
from jax.sharding import PartitionSpec as P

BLK = 128
CBD = 2
PB = 8
MBR = 2
KIDS = 8


def broadcast(shard, axis, root):
    mine = lax.axis_index(axis) == root
    return lax.psum(jnp.where(mine, shard, jnp.zeros_like(shard)), axis)


def solve_rows(inverse, rows_in):
    return lax.dot_general(
        rows_in,
        inverse,
        (((1,), (1,)), ((), ())),
        precision=lax.Precision.HIGHEST,
        preferred_element_type=jnp.float32,
    )


def local(front, children, child_map):
    rows_here, width = front.shape
    row_count = lax.axis_size("row")
    row_index = lax.axis_index("row")
    owner_index = lax.axis_index(("sub", "col"))
    row_blocks = rows_here // BLK
    panel_width = PB * BLK
    kids_here, update_rows, update_cols = children.shape
    sub_count = update_cols // width
    pieces = children.reshape(kids_here, update_rows, sub_count, width)
    arrived = lax.all_to_all(pieces, "sub", split_axis=2, concat_axis=0, tiled=True)
    arrived = arrived.reshape(KIDS * MBR, BLK * width)
    mine = lax.dynamic_slice_in_dim(child_map, row_index * MBR, MBR, 1)
    slot_ids = (mine // row_count).reshape(KIDS * MBR)
    onehot = (jnp.arange(row_blocks, dtype=jnp.int32)[:, None] == slot_ids[None, :]).astype(
        jnp.float32
    )
    added = jnp.dot(
        onehot, arrived, precision=lax.Precision.HIGHEST, preferred_element_type=jnp.float32
    )
    assembled = front + added.reshape(rows_here, width)
    lead_block = assembled[:, :BLK]
    panel_parts = []
    for block_id in range(PB):
        panel_parts.append(broadcast(lead_block, ("sub", "col"), block_id))
    panel = jnp.concatenate(panel_parts, axis=1)
    per_row = PB // row_count
    corner = lax.all_gather(panel[: per_row * BLK], "row", axis=0, tiled=True)
    corner = (
        corner.reshape(row_count, per_row, BLK, panel_width)
        .transpose(1, 0, 2, 3)
        .reshape(panel_width, panel_width)
    )
    factor = jnp.linalg.cholesky(0.5 * (corner + corner.T))
    identity_matrix = jnp.eye(panel_width, dtype=jnp.float32)
    inverse = jax.scipy.linalg.solve_triangular(factor, identity_matrix, lower=True)
    lower_rows = solve_rows(inverse, panel)
    head_blocks = factor.reshape(per_row, row_count, BLK, panel_width)
    own_head = lax.dynamic_index_in_dim(head_blocks, row_index, 1, keepdims=False).reshape(
        per_row * BLK, panel_width
    )
    lower_rows = jnp.concatenate([own_head, lower_rows[per_row * BLK :]], axis=0)
    stride = row_blocks // CBD
    grouped = lower_rows.reshape(CBD, stride, BLK, panel_width)
    picked = lax.dynamic_index_in_dim(grouped, owner_index // row_count, 1, keepdims=False)
    across = broadcast(picked, "row", owner_index % row_count).reshape(CBD * BLK, panel_width)
    product = lax.dot_general(
        lower_rows,
        across,
        (((1,), (1,)), ((), ())),
        precision=lax.Precision.HIGHEST,
        preferred_element_type=jnp.float32,
    )
    result = assembled - product
    block_front = jnp.arange(row_blocks, dtype=jnp.int32) * row_count + row_index
    keep_rows = jnp.repeat((block_front >= PB).astype(jnp.float32), BLK)
    result = result * keep_rows[:, None]
    column_start = jnp.minimum(owner_index, PB - 1) * BLK
    panel_piece = lax.dynamic_slice_in_dim(lower_rows, column_start, BLK, 1)
    first_block = jnp.where(owner_index < PB, panel_piece, result[:, :BLK])
    return jnp.concatenate([first_block, result[:, BLK:]], axis=1)


def solution(mesh):
    placed = (P("row", ("sub", "col")), P("sub", "row", "col"), P())
    return jax.shard_map(
        local, mesh=mesh, in_specs=placed, out_specs=P("row", ("sub", "col")), check_vma=False
    )
```

profile of v0, /device:TPU:2, one launch (start us, length us, event | category | flops | bytes accessed | tf_op | source)
XLA Modules:
  0.0 726.4 jit_solution(1562447247933679191)
XLA Ops:
  6.5 3.2 copy.24
  9.7 4.5 all-to-all-start
  14.3 1.6 copy.11
  15.9 25.5 %all-to-all-done = f32[2,256,4,256]{3,1,0,2:T(8,128)S(1)} async-done(((f32[2,256,4,256]{3,1,0,2:T(8,128)}), f32[2,256,4,256]{3,1,0,2:T(8,128)S(1)}, u32[]{:S(2)}, u32[]{:S(2)}) %all-to-all-start) | async-done | bytes 2097184 | tf_op jit(solution)/shard_map/all_to_all | solution.py:38
  41.4 1.5 reshape.104
  42.9 2.4 fusion.76
  48.1 2.1 slice_select_fusion
  50.3 123.0 %all-reduce.7.cloned.1.call-done = (f32[1024,128]{0,1:T(8,128)}, f32[1024,128]{0,1:T(8,128)}, f32[1024,128]{0,1:T(8,128)}, f32[1024,128]{0,1:T(8,128)}, f32[1024...) async-done(((f32[1024,128]{0,1:T(8,128)}, f32[1024,128]{0,1:T(8,128)}, f32[1024,128]{0,1:T(8,128)}, f32[1024,128]{0,1:T(8,128)}, ...) | async-done | bytes 4194320 | tf_op jit(solution)/shard_map/psum | solution.py:15
  178.0 1.9 copy-done.8
  181.2 2.5 fusion.26
  183.7 59.5 %all-gather.2.cloned.1.call-done = f32[1024,1024]{0,1:T(8,128)} async-done(((f32[128,1024]{0,1:T(8,128)}), f32[1024,1024]{0,1:T(8,128)}) %all-gather.2.cloned.1.call-update) | async-done | bytes 4194320 | tf_op jit(solution)/shard_map/all_gather | solution.py:55
  243.2 5.4 copy.13
  248.5 6.8 fusion.1
  255.4 5.8 copy.14
  261.2 4.4 fusion
  265.6 2.0 copy-done.3
  267.6 11.7 %cholesky.223 = f32[128,128]{1,0:T(8,128)S(1)} custom-call(f32[128,128]{1,0:T(8,128)S(1)} %cholesky.580), custom_call_target="Cholesky" | custom-call | tf_op jit(solution)/shard_map/jit(cholesky)/cholesky | solution.py:61
  279.3 9.8 %custom-call.63 = f32[1,128,128]{1,2,0:T(8,128)S(1)} custom-call(f32[1,128,128]{2,1,0:T(8,128)S(1)} %get-tuple-element.89), custom_call_target="InvertDiagBlocksLowerTriangular" | custom-call | tf_op jit(solution)/shard_map/jit(cholesky)/cholesky | solution.py:61
  289.2 2.5 cholesky.255
  291.7 2.4 constant_dynamic-update-slice_fusion.33
  295.6 11.9 %cholesky.244 = f32[128,128]{1,0:T(8,128)S(1)} custom-call(f32[128,128]{1,0:T(8,128)S(1)} %cholesky.584), custom_call_target="Cholesky" | custom-call | tf_op jit(solution)/shard_map/jit(cholesky)/cholesky | solution.py:61
  308.1 9.8 %custom-call.64 = f32[1,128,128]{1,2,0:T(8,128)S(1)} custom-call(f32[1,128,128]{2,1,0:T(8,128)S(1)} %get-tuple-element.86), custom_call_target="InvertDiagBlocksLowerTriangular" | custom-call | tf_op jit(solution)/shard_map/jit(cholesky)/cholesky | solution.py:61
  319.2 2.1 convolution_subtract_fusion.7
  321.3 11.7 %cholesky.468 = f32[128,128]{1,0:T(8,128)S(1)} custom-call(f32[128,128]{1,0:T(8,128)S(1)} %cholesky.589), custom_call_target="Cholesky" | custom-call | tf_op jit(solution)/shard_map/jit(cholesky)/cholesky | solution.py:61
  334.4 9.8 %custom-call.65 = f32[1,128,128]{1,2,0:T(8,128)S(1)} custom-call(f32[1,128,128]{2,1,0:T(8,128)S(1)} %get-tuple-element.83), custom_call_target="InvertDiagBlocksLowerTriangular" | custom-call | tf_op jit(solution)/shard_map/jit(cholesky)/cholesky | solution.py:61
  345.4 2.3 convolution_subtract_fusion.8
  347.7 11.9 %cholesky.487 = f32[128,128]{1,0:T(8,128)S(1)} custom-call(f32[128,128]{1,0:T(8,128)S(1)} %cholesky.594), custom_call_target="Cholesky" | custom-call | tf_op jit(solution)/shard_map/jit(cholesky)/cholesky | solution.py:61
  361.0 9.8 %custom-call.66 = f32[1,128,128]{1,2,0:T(8,128)S(1)} custom-call(f32[1,128,128]{2,1,0:T(8,128)S(1)} %get-tuple-element.80), custom_call_target="InvertDiagBlocksLowerTriangular" | custom-call | tf_op jit(solution)/shard_map/jit(cholesky)/cholesky | solution.py:61
  371.9 2.3 convolution_subtract_fusion.9
  374.2 11.7 %cholesky.506 = f32[128,128]{1,0:T(8,128)S(1)} custom-call(f32[128,128]{1,0:T(8,128)S(1)} %cholesky.599), custom_call_target="Cholesky" | custom-call | tf_op jit(solution)/shard_map/jit(cholesky)/cholesky | solution.py:61
  387.3 10.2 %custom-call.67 = f32[1,128,128]{1,2,0:T(8,128)S(1)} custom-call(f32[1,128,128]{2,1,0:T(8,128)S(1)} %get-tuple-element.77), custom_call_target="InvertDiagBlocksLowerTriangular" | custom-call | tf_op jit(solution)/shard_map/jit(cholesky)/cholesky | solution.py:61
  398.5 2.3 convolution_subtract_fusion.10
  400.8 11.7 %cholesky.526 = f32[128,128]{1,0:T(8,128)S(1)} custom-call(f32[128,128]{1,0:T(8,128)S(1)} %cholesky.604), custom_call_target="Cholesky" | custom-call | tf_op jit(solution)/shard_map/jit(cholesky)/cholesky | solution.py:61
  413.9 9.8 %custom-call.68 = f32[1,128,128]{1,2,0:T(8,128)S(1)} custom-call(f32[1,128,128]{2,1,0:T(8,128)S(1)} %get-tuple-element.74), custom_call_target="InvertDiagBlocksLowerTriangular" | custom-call | tf_op jit(solution)/shard_map/jit(cholesky)/cholesky | solution.py:61
  424.6 2.0 convolution_subtract_fusion.11
  426.7 11.9 %cholesky.546 = f32[128,128]{1,0:T(8,128)S(1)} custom-call(f32[128,128]{1,0:T(8,128)S(1)} %cholesky.609), custom_call_target="Cholesky" | custom-call | tf_op jit(solution)/shard_map/jit(cholesky)/cholesky | solution.py:61
  439.8 9.8 %custom-call.69 = f32[1,128,128]{1,2,0:T(8,128)S(1)} custom-call(f32[1,128,128]{2,1,0:T(8,128)S(1)} %get-tuple-element.71), custom_call_target="InvertDiagBlocksLowerTriangular" | custom-call | tf_op jit(solution)/shard_map/jit(cholesky)/cholesky | solution.py:61
  450.4 1.8 convolution_subtract_fusion.12
  452.2 11.7 %cholesky.564 = f32[128,128]{1,0:T(8,128)S(1)} custom-call(f32[128,128]{1,0:T(8,128)S(1)} %convolution_subtract_fusion.12), custom_call_target="Cholesky" | custom-call | tf_op jit(solution)/shard_map/jit(cholesky)/cholesky | solution.py:61
  470.9 4.9 fusion.2
  476.0 27.9 %while.1 = (s32[]{:T(128)}, f32[1024,1024]{1,0:T(8,128)}, s32[8,2]{0,1:T(2,128)S(1)}, f32[8,128,128]{2,1,0:T(8,128)}, s32[]{:T(128)}) while((s32[]{:T(128)}, f32[1024,1024]{1,0:T(8,128)}, s32[8,2]{0,1:T(2,128)S(1)}, f32[8,128,128]{2,1,0:T(8,128)}, s32[]{:T(128)}) %tuple.66), condition=%wide.while_cond, body=%wide.while_body.sunk | while | flops 2 | bytes 132205 | solution.py:63
  476.7 2.9 bitcast_dynamic-update-slice_fusion.2
  480.1 2.9 bitcast_dynamic-update-slice_fusion.2
  483.6 2.9 bitcast_dynamic-update-slice_fusion.2
  487.1 2.9 bitcast_dynamic-update-slice_fusion.2
  490.6 2.9 bitcast_dynamic-update-slice_fusion.2
  494.1 2.9 bitcast_dynamic-update-slice_fusion.2
  497.6 2.9 bitcast_dynamic-update-slice_fusion.2
  501.1 2.8 bitcast_dynamic-update-slice_fusion.2
  503.9 79.6 %custom-call.70 = f32[8,128,128]{1,2,0:T(8,128)S(1)} custom-call(f32[8,128,128]{2,1,0:T(8,128)} %get-tuple-element.12), custom_call_target="InvertDiagBlocksLowerTriangular" | custom-call | tf_op jit(solution)/shard_map/jit(_solve_triangular)/triangular_solve | solution.py:63
  584.1 1.9 convolution_subtract_fusion.5
  586.7 1.6 convolution_subtract_fusion.1
  589.1 2.0 fusion.20
  591.9 2.2 fusion.23
  594.9 2.6 convolution_subtract_fusion.3
  598.2 2.8 convolution_subtract_fusion.2
  601.7 4.0 convolution_subtract_fusion.4
  606.4 13.6 %fusion.3 = f32[896,1024]{0,1:T(8,128)S(1)} fusion(f32[1024,1024]{1,0:T(8,128)S(1)} %convolution_dynamic-update-slice_fusion, f32[1024,1024]{0,1:T(8,128)S(1)} %copy-done.9), kind=kOutput, calls=%fused_computation.13 | convolution fusion | flops 11274289152 | bytes 11534336 | tf_op jit(solution)/shard_map/dot_general | solution.py:19
  620.0 1.9 copy-done
  621.9 2.5 pad_maximum_fusion
  624.4 5.6 reshape.108
  630.0 6.0 fusion.27
  637.2 74.7 %all-reduce.5.cloned.1.call-done = f32[256,1024]{0,1:T(8,128)} async-done(((f32[256,1024]{0,1:T(8,128)}), f32[256,1024]{0,1:T(8,128)}) %all-reduce.5.cloned.1.call-update) | async-done | bytes 1048592 | tf_op jit(solution)/shard_map/psum | solution.py:15
  711.8 6.3 fusion.19
  (104 shorter events, 39.3 us)
Async XLA Ops:
  6.5 7.6 %copy-start.10 = (s32[8,16]{1,0:T(8,128)S(1)}, s32[8,16]{1,0:T(8,128)}, u32[]{:S(2)}) copy-start(s32[8,16]{1,0:T(8,128)} %param.5) | copy-start | bytes 1540
  9.7 31.7 %all-to-all-start = ((f32[2,256,4,256]{3,1,0,2:T(8,128)}), f32[2,256,4,256]{3,1,0,2:T(8,128)S(1)}, u32[]{:S(2)}, u32[]{:S(2)}) async-start(f32[2,256,4,256]{3,1,0,2:T(8,128)} %bitcast.132), calls=%async_computation | async-start | bytes 4194304 | tf_op jit(solution)/shard_map/all_to_all | solution.py:38
  14.2 159.1 %all-reduce.7.cloned.1.call-start = ((), (), s32[]{:S(2)}) async-start(), calls=%async_computation.3 | async-start | bytes 8388608 | tf_op jit(solution)/shard_map/psum | solution.py:15
  50.2 192.9 %all-gather.2.cloned.1.call-start = ((), (), s32[]{:S(2)}) async-start(), calls=%async_computation.1 | async-start | bytes 4718592 | tf_op jit(solution)/shard_map/all_gather | solution.py:55
  173.3 4.5 copy-start.7
  173.3 4.5 copy-start.6
  173.3 4.6 copy-start.5
  173.3 4.7 copy-start.4
  178.0 1.9 copy-start.8
  180.8 531.0 %all-reduce.5.cloned.1.call-start = ((), (), s32[]{:S(2)}) async-start(), calls=%async_computation.2 | async-start | bytes 2097152 | tf_op jit(solution)/shard_map/psum | solution.py:15
  265.6 2.0 copy-start.3
  583.5 3.2 copy-start.2
  601.0 5.3 copy-start.9
  620.0 1.9 copy-start
  711.8 6.3 copy-start.1
Sparse Core Ops, SparseCore 0:
  50.4 122.8 all-reduce.6
  180.9 62.1 all-gather.1
  637.2 74.6 all-reduce.4
where the time goes:
time: 732 us; the launch traced here: 726 us
  other arithmetic  283 us (39%)
  waiting for transfers between devices  283 us (39%)
  local copies, waits for them, and re-layouts  68.9 us (9%)
  matrix products  68.1 us (9%)
  between operations  19 us (3%)
    psum x2, waiting for transfers between devices, broadcast(): return lax.psum(jnp.where(mine, shard, jnp.zeros_like(shard)), axis)  198 us
    another operation x30, other arithmetic, local(): factor = jnp.linalg.cholesky(0.5 * (corner + corner.T))  172 us
    another operation x3, other arithmetic, local(): jax.scipy.linalg.solve_triangular(factor, identity_matrix, lower=True)  84.5 us
    all_gather x1, waiting for transfers between devices, local(): corner = lax.all_gather(panel[:per_row * BLK], 'row', axis=0, tiled=True)  59.5 us
    another operation x24, local copies, waits for them, and re-layouts  27.8 us
    all_to_all x1, waiting for transfers between devices, local(): lax.all_to_all(pieces, 'sub', split_axis=2, concat_axis=0, tiled=True)  25.5 us
    another operation x14, matrix products, local(): factor = jnp.linalg.cholesky(0.5 * (corner + corner.T))  23.1 us
    another operation x15, matrix products, local(): jax.scipy.linalg.solve_triangular(factor, identity_matrix, lower=True)  22.7 us
  transfers between devices with their start and end apart: 4, of which 4 were waited for; matrix products, arithmetic and copies ran while one was open for 1% of the time, Pallas kernels for 0%

commit v1 on v0

v1 whole, which is shorter than its diff:
```python
import functools

import jax
import jax.numpy as jnp
from jax import lax
from jax.experimental import pallas as pl
from jax.experimental.pallas import tpu as pltpu
from jax.sharding import Mesh, PartitionSpec as P

BLK = 128
PB = 8
PW = PB * BLK
KIDS = 8
MBR = 2
NSB = 4
QR = BLK // NSB
f32 = jnp.float32
bf16 = jnp.bfloat16
NT = (((1,), (1,)), ((), ()))
NN = (((1,), (0,)), ((), ()))
SUB = ("yh", "core")
COL = ("yl", "x")
PLANE = SUB + COL
CHIPS = ("yh", "yl", "x")


def split(x):
    hi = x.astype(bf16)
    return hi, (x - hi.astype(f32)).astype(bf16)


def dot3(a, b, dims):
    (ah, al), (bh, bl) = a, b

    def dot(p, q):
        return lax.dot_general(p, q, dims, preferred_element_type=f32)

    return dot(ah, bh) + (dot(ah, bl) + dot(al, bh))


def row_of(x, j):
    return jnp.broadcast_to(x[j : j + 1, :], x.shape)


def col_of(x, j):
    return jnp.broadcast_to(x[:, j : j + 1], x.shape)


def factor_block(d):
    groups = BLK // 8
    rows = lax.broadcasted_iota(jnp.int32, (8, BLK), 0)
    lanes = lax.broadcasted_iota(jnp.int32, (8, BLK), 1)
    a = [d[8 * v : 8 * v + 8, :] for v in range(groups)]
    e = [(lanes == rows + 8 * v).astype(f32) for v in range(groups)]
    upper, inverse = [], []
    for p in range(groups):
        ap, ep = a[p], e[p]
        b = [col_of(ap, 8 * p + j) for j in range(8)]
        near = p + 1 < groups
        bn = [col_of(a[p + 1], 8 * p + j) for j in range(8)] if near else None
        us, es = [], []
        up = jnp.zeros((8, BLK), f32)
        ip = jnp.zeros((8, BLK), f32)
        for j in range(8):
            inv = lax.rsqrt(row_of(b[j], j))
            m = b[j] * inv
            u = row_of(ap, j) * inv
            w = row_of(ep, j) * inv
            us.append(u)
            es.append(w)
            up = jnp.where(rows == j, u, up)
            ip = jnp.where(rows == j, w, ip)
            if j < 7:
                ap = ap - m * u
                ep = ep - m * w
            if near:
                mn = bn[j] * inv
                a[p + 1] = a[p + 1] - mn * u
                e[p + 1] = e[p + 1] - mn * w
            for k in range(j + 1, 8):
                mk = row_of(m, k)
                b[k] = b[k] - m * mk
                if near:
                    bn[k] = bn[k] - mn * mk
        upper.append(up)
        inverse.append(ip)
        if p + 2 < groups:
            lt = up.T
            for v in range(p + 2, groups):
                lv = lt[8 * v : 8 * v + 8, :]
                av, ev = a[v], e[v]
                for j in range(8):
                    m = jnp.broadcast_to(lv[:, j : j + 1], (8, BLK))
                    av = av - m * us[j]
                    ev = ev - m * es[j]
                a[v], e[v] = av, ev
    return jnp.concatenate(upper, 0), jnp.concatenate(inverse, 0)


def corner_kernel(ids, own_ref, other_ref, piece_ref, xh_ref, xl_ref, c_ref, l_ref, lh_ref, ll_ref):
    nb = PB
    core, row, owner = ids[0], ids[1], ids[2]

    def at(i, n=1):
        return slice(i * BLK, (i + n) * BLK)

    for yh in range(2):
        for c in range(PB):
            for i in range(PB):
                base = i * BLK + yh * 2 * QR
                rows = slice(i * QR, (i + 1) * QR)
                c_ref[pl.ds(pl.multiple_of(base + core * QR, QR), QR), at(c)] = own_ref[yh * PB + c, rows, :]
                c_ref[pl.ds(pl.multiple_of(base + (1 - core) * QR, QR), QR), at(c)] = other_ref[yh * PB + c, rows, :]

    def sym(i, j):
        return 0.5 * (c_ref[at(i), at(j)] + c_ref[at(j), at(i)].T)

    def get(rows, cols):
        return lh_ref[rows, cols], ll_ref[rows, cols]

    def put(rows, cols, x):
        h, l = split(x)
        l_ref[rows, cols] = x
        lh_ref[rows, cols] = h
        ll_ref[rows, cols] = l
        return h, l

    def putx(rows, cols, x):
        h, l = split(x)
        xh_ref[rows, cols] = h
        xl_ref[rows, cols] = l

    r = lax.broadcasted_iota(jnp.int32, (BLK, BLK), 0)
    c = lax.broadcasted_iota(jnp.int32, (BLK, BLK), 1)
    d = sym(0, 0)
    zero = jnp.zeros((BLK, BLK), f32)
    zb = zero.astype(bf16)
    wp = panel = m = None
    for k in range(nb):
        below = nb - 1 - k
        cols = slice(0, k * BLK)
        if k >= 1:
            if below > 0:
                put(at(k + 1, below), at(k - 1), dot3(split(panel[BLK:]), wp, NT))
            if k >= 2:
                putx(at(k - 1), slice(0, (k - 1) * BLK), -dot3(wp, split(m), NN))
            m = dot3(get(at(k), cols), (xh_ref[cols, cols], xl_ref[cols, cols]), NN)
        if below > 0:
            panel = jnp.concatenate([sym(i, k) for i in range(k + 1, nb)], 0)
            dn = sym(k + 1, k + 1)
            if k >= 1:
                panel = panel - dot3(get(at(k + 1, below), cols), get(at(k), cols), NT)
                nx = get(at(k + 1), cols)
                dn = dn - dot3(nx, nx, NT)
        u, w = factor_block(d)
        l_ref[at(k), at(k)] = jnp.where(r >= c, u.T, zero)
        wp = split(w)
        xh_ref[at(k), at(k)], xl_ref[at(k), at(k)] = wp
        for j in range(k + 1, nb):
            l_ref[at(k), at(j)] = zero
            xh_ref[at(k), at(j)] = zb
            xl_ref[at(k), at(j)] = zb
        if below > 0:
            nxt = put(at(k + 1), at(k), dot3(split(panel[:BLK]), wp, NT))
            d = dn - dot3(nxt, nxt, NT)
    putx(at(nb - 1), slice(0, (nb - 1) * BLK), -dot3(wp, split(m), NN))
    place = pl.multiple_of(jnp.minimum(owner, PB - 1) * BLK, BLK)
    piece_ref[...] = l_ref[pl.ds(pl.multiple_of(row * BLK, BLK), BLK), pl.ds(place, BLK)]


def corner_step(ids, own, other):
    vm = pl.BlockSpec(memory_space=pltpu.VMEM)
    return pl.pallas_call(
        corner_kernel,
        out_shape=(
            jax.ShapeDtypeStruct((BLK, BLK), f32),
            jax.ShapeDtypeStruct((PW, PW), bf16),
            jax.ShapeDtypeStruct((PW, PW), bf16),
        ),
        in_specs=[pl.BlockSpec(memory_space=pltpu.SMEM), vm, vm],
        out_specs=[vm] * 3,
        scratch_shapes=[pltpu.VMEM((PW, PW), f32)] * 2 + [pltpu.VMEM((PW, PW), bf16)] * 2,
        compiler_params=pltpu.CompilerParams(vmem_limit_bytes=40 * 1024 * 1024),
        cost_estimate=pl.CostEstimate(flops=60_000_000_000, bytes_accessed=8 * PW * PW, transcendentals=PW),
        name="corner",
    )(ids, own, other)


def tail_kernel(ids, slots, front_ref, kids_ref, own_ref, other_ref, tc_ref, piece_ref, xh_ref, xl_ref, out_ref, th_ref, tl_ref, ch_ref, cl_ref):
    core, row, owner = ids[0], ids[1], ids[2]
    width = 2 * BLK

    def at(i, n=1):
        return slice(i * BLK, (i + n) * BLK)

    for yh in range(2):
        for c in range(PB):
            for which, ref in ((core, own_ref), (1 - core, other_ref)):
                for i in range(1, PB):
                    h, l = split(ref[yh * PB + c, (i - 1) * QR : i * QR, :])
                    rows = pl.ds(pl.multiple_of(i * BLK + yh * 2 * QR + which * QR, QR), QR)
                    th_ref[rows, at(c)] = h
                    tl_ref[rows, at(c)] = l
    for q in range(NSB):
        for c in range(PB):
            for g in range(2):
                h, l = split(tc_ref[q * PB + c, g * QR : (g + 1) * QR, :])
                rows = slice(g * BLK + q * QR, g * BLK + (q + 1) * QR)
                ch_ref[rows, at(c)] = h
                cl_ref[rows, at(c)] = l
    out_ref[...] = front_ref[...]
    for b in range(KIDS * MBR):
        rows = pl.ds(pl.multiple_of(slots[b] * BLK, BLK), BLK)
        out_ref[rows, :] += kids_ref[b]
    x = (xh_ref[...], xl_ref[...])
    y = dot3((ch_ref[...], cl_ref[...]), x, NT)
    z = split(dot3(split(y), x, NN))
    for i in range(1, PB):
        t = (th_ref[at(i), :], tl_ref[at(i), :])
        out_ref[at(i), :] -= dot3(t, z, NT)
    out_ref[at(0), :] = jnp.zeros((BLK, width), f32)

    @pl.when(owner < PB)
    def _():
        block = pl.ds(pl.multiple_of(jnp.minimum(owner, PB - 1) * BLK, BLK), BLK)
        xb = (xh_ref[block, :], xl_ref[block, :])
        out_ref[at(0), at(0)] = piece_ref[...]
        for i in range(1, PB):
            out_ref[at(i), at(0)] = dot3((th_ref[at(i), :], tl_ref[at(i), :]), xb, NT)


def tail_step(ids, slots, front, kids, own, other, tall_cols, piece, xh, xl):
    vm = pl.BlockSpec(memory_space=pltpu.VMEM)
    sm = pl.BlockSpec(memory_space=pltpu.SMEM)
    return pl.pallas_call(
        tail_kernel,
        out_shape=jax.ShapeDtypeStruct(front.shape, f32),
        in_specs=[sm, sm] + [vm] * 8,
        out_specs=vm,
        scratch_shapes=[pltpu.VMEM((PW, PW), bf16)] * 2 + [pltpu.VMEM((2 * BLK, PW), bf16)] * 2,
        compiler_params=pltpu.CompilerParams(vmem_limit_bytes=40 * 1024 * 1024),
        cost_estimate=pl.CostEstimate(flops=6_000_000_000, bytes_accessed=20 * PW * PW, transcendentals=0),
        name="tail",
    )(ids, slots, front, kids, own, other, tall_cols, piece, xh, xl)


def to_all(x, axes, count):
    return lax.all_to_all(jnp.broadcast_to(x[None], (count,) + x.shape), axes, 0, 0, tiled=True)


def other_core(x):
    return lax.ppermute(x, "core", [(0, 1), (1, 0)])


def local(front, children, child_map):
    row = lax.axis_index("row")
    sub = lax.axis_index(SUB)
    col = lax.axis_index(COL)
    owner = sub * PB + col
    ids = jnp.stack([lax.axis_index("core"), row, owner]).astype(jnp.int32)
    width = front.shape[1]
    mine = lax.dynamic_slice_in_dim(child_map, row * MBR, MBR, 1) // PB
    slots = mine.reshape(KIDS * MBR)
    here = lax.dynamic_slice_in_dim(mine, sub * 2, 2, 0).reshape(4)

    lead = children[:, :, :BLK].reshape(4, BLK, BLK)
    part = jnp.where(sub == 0, front[:BLK, :BLK], 0.0)
    for b in range(4):
        part = part + jnp.where(here[b] == 0, lead[b], 0.0)
    quarter = lax.all_to_all(part.reshape(NSB, QR, BLK), SUB, 0, 0, tiled=True).sum(0)
    column = to_all(quarter, "row", 8)
    c_own = to_all(column.reshape(8 * QR, BLK), CHIPS, 16)
    c_other = other_core(c_own)
    piece, xh, xl = corner_step(ids, c_own, c_other)

    kid_part = lead.reshape(4, NSB, QR, BLK).transpose(1, 0, 2, 3)
    front_part = front[:, :BLK].reshape(PB, NSB, QR, BLK).transpose(1, 0, 2, 3)
    came = lax.all_to_all(jnp.concatenate([kid_part, front_part], 1), SUB, 0, 0, tiled=True)
    onehot = (jnp.arange(PB, dtype=jnp.int32)[:, None] == slots[None, :]).astype(f32)
    summed = jnp.dot(
        onehot,
        came[:, :4].reshape(KIDS * MBR, QR * BLK),
        precision=lax.Precision.HIGHEST,
        preferred_element_type=f32,
    )
    tall = came[0, 4:] + summed.reshape(PB, QR, BLK)
    t_own = to_all(tall[1:].reshape(7 * QR, BLK), CHIPS, 16)
    t_other = other_core(t_own)
    along = to_all(tall, "row", 8).reshape(8, 2, NSB, QR, BLK)
    pieces = along.transpose(2, 0, 1, 3, 4).reshape(NSB * 8, 2 * QR, BLK)
    tall_cols = lax.all_to_all(pieces, PLANE, 0, 0, tiled=True)

    parts = children.reshape(2, MBR * BLK, NSB, width)
    kids = lax.all_to_all(parts, SUB, split_axis=2, concat_axis=0, tiled=True)
    kids = kids.reshape(KIDS * MBR, BLK, width)
    return tail_step(ids, slots, front, kids, t_own, t_other, tall_cols, piece, xh, xl)


def solution(mesh):
    fine = Mesh(mesh.devices.reshape(2, 2, 8, 2, 4), ("yh", "core", "row", "yl", "x"))
    placed = (P("row", PLANE), P(SUB, "row", COL), P())
    return jax.shard_map(
        local, mesh=fine, in_specs=placed, out_specs=P("row", PLANE), check_vma=False
    )
```

time: 732 us -> 257 us (0.35)
  other arithmetic: 283 us -> 1.85 us
  waiting for transfers between devices: 283 us -> 108 us
  matrix products: 68.1 us -> 0.37 us
  Pallas kernels: 0 us -> 58.1 us
  local copies, waits for them, and re-layouts: 68.9 us -> 17.9 us
  starting transfers between devices: 4.55 us -> 38.2 us
  blocking collectives: 0 us -> 25.4 us
  between operations: 19 us -> 3.06 us
    another operation x33 -> x1, other arithmetic: 257 us -> 0.08 us  [local(): ids = jnp.stack([lax.axis_index('core'), row, owner]).astype(jnp.int32)]
    psum x2 -> x0, waiting for transfers between devices: 198 us -> none  [broadcast(): return lax.psum(jnp.where(mine, shard, jnp.zeros_like(shard)), axis)]
    all_to_all x1 -> x6, waiting for transfers between devices: 25.5 us -> 108 us  [the longest x4 82.1 us: to_all(): lax.all_to_all(jnp.broadcast_to(x[None], (count,) + x.shape), axes, 0, 0,...]
    all_gather x1 -> x0, waiting for transfers between devices: 59.5 us -> none  [local(): corner = lax.all_gather(panel[:per_row * BLK], 'row', axis=0, tiled=True)]
    pallas_call x0 -> x2, Pallas kernels: none -> 58.1 us  [the longest x1 44.4 us: corner_step(): pl.pallas_call(corner_kernel, out_shape=(jax.ShapeDtypeStruct((BLK, BLK),...]
    another operation x29 -> x0, matrix products: 45.8 us -> none  [the longest x14 23.1 us: local(): factor = jnp.linalg.cholesky(0.5 * (corner + corner.T))]
    all_to_all x1 -> x6, starting transfers between devices: 4.46 us -> 37.7 us  [the longest x4 25.3 us: to_all(): lax.all_to_all(jnp.broadcast_to(x[None], (count,) + x.shape), axes, 0, 0,...]
    another operation x33 -> x0, local copies, waits for them, and re-layouts: 30.4 us -> none
  transfers between devices with their start and end apart: 4 -> 8, of which waited for: 4 -> 5; matrix products, arithmetic and copies ran while one was open for 1% -> 2% of each run, Pallas kernels for 0% -> 18%
where the time goes in v1:
time: 257 us; the launch traced here: 253 us
  waiting for transfers between devices  108 us (42%)
  Pallas kernels  58.1 us (23%)
  starting transfers between devices  38.2 us (15%)
  blocking collectives  25.4 us (10%)
  local copies, waits for them, and re-layouts  17.9 us (7%)
  between operations  3.06 us (1%)
    all_to_all x4, waiting for transfers between devices, to_all(): lax.all_to_all(jnp.broadcast_to(x[None], (count,) + x.shape), axes, 0, 0,...  82.1 us
    pallas_call x1, Pallas kernels, corner_step(): pl.pallas_call(corner_kernel, out_shape=(jax.ShapeDtypeStruct((BLK, BLK),...  44.4 us
    all_to_all x1, waiting for transfers between devices, local(): kids = lax.all_to_all(parts, SUB, split_axis=2, concat_axis=0, tiled=True)  25.6 us
    all_to_all x4, starting transfers between devices, to_all(): lax.all_to_all(jnp.broadcast_to(x[None], (count,) + x.shape), axes, 0, 0,...  25.3 us
    all_to_all x1, blocking collectives, local(): lax.all_to_all(jnp.concatenate([kid_part, front_part], 1), SUB, 0, 0, til...  15.6 us
    pallas_call x1, Pallas kernels, tail_step(): pl.pallas_call(tail_kernel, out_shape=jax.ShapeDtypeStruct(front.shape, f...  13.7 us
    all_to_all x1, blocking collectives, local(): lax.all_to_all(part.reshape(NSB, QR, BLK), SUB, 0, 0, tiled=True).sum(0)  9.89 us
    all_to_all x1, starting transfers between devices, local(): tall_cols = lax.all_to_all(pieces, PLANE, 0, 0, tiled=True)  7.93 us
  transfers between devices with their start and end apart: 8, of which 5 were waited for; matrix products, arithmetic and copies ran while one was open for 2% of the time, Pallas kernels for 18%

profile of v1, /device:TPU:2, one launch (start us, length us, event | category | flops | bytes accessed | tf_op | source)
XLA Modules:
  0.0 252.7 jit_solution(2439659214946439523)
XLA Ops:
  0.0 0.0 slice-start
  0.0 0.8 add_select_fusion
  0.8 0.1 reshape.65
  0.9 0.6 fusion.15
  4.0 1.0 slice.42
  5.0 0.9 fusion.3
  5.8 9.9 %all_to_all.50 = f32[4,32,128]{2,1,0:T(8,128)S(1)} all-to-all(f32[4,32,128]{2,1,0:T(8,128)S(1)} %bitcast.83), channel_id=1, replica_groups=mesh['yh'=2,'core'=2,'row'=8,'yl'=2,'x'=4] {'yh','core'}, dimensions={0} | all-to-all | bytes 131072 | tf_op jit(solution)/shard_map/all_to_all | solution.py:270
  15.7 0.7 broadcast_in_dim.42
  16.4 8.5 %all-to-all-start.6 = ((f32[8,32,128]{2,1,0:T(8,128)}), f32[8,32,128]{2,1,0:T(8,128)S(1)}, u32[]{:S(2)}, u32[]{:S(2)}) async-start(f32[8,32,128]{2,1,0:T(8,128)} %broadcast_in_dim.42), calls=%async_computation.6 | async-start | bytes 262144 | tf_op jit(solution)/shard_map/all_to_all | solution.py:248
  24.9 0.0 slice-done
  24.9 0.1 pad_maximum_fusion
  25.0 0.1 copy.15
  25.0 8.9 %all-to-all-done.6 = f32[8,32,128]{2,1,0:T(8,128)S(1)} async-done(((f32[8,32,128]{2,1,0:T(8,128)}), f32[8,32,128]{2,1,0:T(8,128)S(1)}, u32[]{:S(2)}, u32[]{:S(2)}) %all-to-all-start.6) | async-done | bytes 131104 | tf_op jit(solution)/shard_map/all_to_all | solution.py:248
  33.9 15.6 %all_to_all.51 = f32[4,12,32,128]{3,2,1,0:T(8,128)S(1)} all-to-all(f32[4,12,32,128]{3,2,1,0:T(8,128)S(1)} %copy.15), channel_id=1, replica_groups=mesh['yh'=2,'core'=2,'row'=8,'yl'=2,'x'=4] {'yh','core'}, dimensions={0} | all-to-all | bytes 1572864 | tf_op jit(solution)/shard_map/all_to_all | solution.py:278
  49.5 1.5 broadcast_in_dim.44
  51.0 5.0 %all-to-all-start.7 = ((f32[16,256,128]{2,1,0:T(8,128)}), f32[16,256,128]{2,1,0:T(8,128)S(1)}, u32[]{:S(2)}, u32[]{:S(2)}) async-start(f32[16,256,128]{2,1,0:T(8,128)} %broadcast_in_dim.44), calls=%async_computation.7 | async-start | bytes 4194304 | tf_op jit(solution)/shard_map/all_to_all | solution.py:248
  56.0 0.1 reshape.58.slots
  56.1 0.4 convolution_add_fusion
  56.6 26.3 %all-to-all-done.7.own_ref = f32[16,256,128]{2,1,0:T(8,128)S(1)} async-done(((f32[16,256,128]{2,1,0:T(8,128)}), f32[16,256,128]{2,1,0:T(8,128)S(1)}, u32[]{:S(2)}, u32[]{:S(2)}) %all-to-all-start.7) | async-done | bytes 2097184 | tf_op jit(solution)/shard_map/all_to_all | solution.py:248
  82.9 1.4 broadcast_in_dim.38
  84.3 8.3 %all-to-all-start.2 = ((f32[16,224,128]{2,1,0:T(8,128)}), f32[16,224,128]{2,1,0:T(8,128)}, u32[]{:S(2)}, u32[]{:S(2)}) async-start(f32[16,224,128]{2,1,0:T(8,128)} %broadcast_in_dim.38), calls=%async_computation.2 | async-start | bytes 3670016 | tf_op jit(solution)/shard_map/all_to_all | solution.py:248
  92.7 23.4 %all-to-all-done.2.own_ref = f32[16,224,128]{2,1,0:T(8,128)} async-done(((f32[16,224,128]{2,1,0:T(8,128)}), f32[16,224,128]{2,1,0:T(8,128)}, u32[]{:S(2)}, u32[]{:S(2)}) %all-to-all-start.2) | async-done | bytes 1835040 | tf_op jit(solution)/shard_map/all_to_all | solution.py:248
  116.1 1.1 broadcast_in_dim.39
  117.1 3.6 %all-to-all-start.3 = ((f32[8,8,32,128]{3,2,1,0:T(8,128)}), f32[8,8,32,128]{3,2,1,0:T(8,128)S(1)}, u32[]{:S(2)}, u32[]{:S(2)}) async-start(f32[8,8,32,128]{3,2,1,0:T(8,128)} %broadcast_in_dim.39), calls=%async_computation.3 | async-start | bytes 2097152 | tf_op jit(solution)/shard_map/all_to_all | solution.py:248
  120.7 0.1 collective-permute-start.1
  120.8 3.1 %copy.36 = f32[2,32,4,8,256]{4,3,1,0,2:T(8,128)} copy(f32[2,32,4,8,256]{4,3,2,1,0:T(8,128)} %bitcast.77) | data formatting | bytes 4194304 | tf_op jit(solution)/shard_map/reshape | solution.py:293
  124.0 23.5 %all-to-all-done.3 = f32[8,8,32,128]{3,2,1,0:T(8,128)S(1)} async-done(((f32[8,8,32,128]{3,2,1,0:T(8,128)}), f32[8,8,32,128]{3,2,1,0:T(8,128)S(1)}, u32[]{:S(2)}, u32[]{:S(2)}) %all-to-all-start.3) | async-done | bytes 1048608 | tf_op jit(solution)/shard_map/all_to_all | solution.py:248
  147.5 4.4 %all-to-all-start = ((f32[2,256,4,256]{3,1,0,2:T(8,128)}), f32[2,256,4,256]{3,1,0,2:T(8,128)}, u32[]{:S(2)}, u32[]{:S(2)}) async-start(f32[2,256,4,256]{3,1,0,2:T(8,128)} %bitcast.74), calls=%async_computation | async-start | bytes 4194304 | tf_op jit(solution)/shard_map/all_to_all | solution.py:294
  151.9 0.1 pad_add_fusion.ids
  152.0 0.5 collective-permute-start
  152.5 1.1 copy.20
  153.5 25.6 %all-to-all-done = f32[2,256,4,256]{3,1,0,2:T(8,128)} async-done(((f32[2,256,4,256]{3,1,0,2:T(8,128)}), f32[2,256,4,256]{3,1,0,2:T(8,128)}, u32[]{:S(2)}, u32[]{:S(2)}) %all-to-all-start) | async-done | bytes 2097184 | tf_op jit(solution)/shard_map/all_to_all | solution.py:294
  179.2 7.9 %all-to-all-start.4 = ((f32[32,64,128]{2,1,0:T(8,128)}), f32[32,64,128]{2,1,0:T(8,128)S(1)}, u32[]{:S(2)}, u32[]{:S(2)}) async-start(f32[32,64,128]{2,1,0:T(8,128)} %bitcast.76), calls=%async_computation.4 | async-start | bytes 2097152 | tf_op jit(solution)/shard_map/all_to_all | solution.py:291
  187.1 0.0 collective-permute-done.1.other_ref
  187.1 44.4 %corner.1 = (f32[128,128]{1,0:T(8,128)S(1)}, bf16[1024,1024]{1,0:T(8,128)(2,1)S(1)}, bf16[1024,1024]{1,0:T(8,128)(2,1)S(1)}) custom-call(s32[3]{0:T(128)S(1)} %pad_add_fusion.ids, f32[16,256,128]{2,1,0:T(8,128)S(1)} %all-to-all-done.7.own_ref, f32[16,256,128]{2,1,0:T(8,128)} %collective-permute-done.1.other_ref), custom_call_target="tpu_custom_call" | custom-call | flops 60000002048 | bytes 8388608 | tf_op jit(solution)/shard_map/corner/pallas_call | solution.py:173
  231.5 0.0 copy-start.1
  231.5 1.3 copy-done.1
  232.8 0.0 copy-start.3
  232.8 1.4 copy-done.3
  234.2 0.0 all-to-all-done.4.tc_ref
  234.2 0.0 collective-permute-done.other_ref
  234.2 0.0 copy-start
  234.2 1.2 copy-done
  235.4 0.0 copy-start.2
  235.4 1.6 copy-done.2
  237.0 0.0 copy-start.4
  237.0 1.6 copy-done.4
  238.6 13.7 %tail.1 = f32[1024,256]{1,0:T(8,128)} custom-call(s32[3]{0:T(128)S(1)} %pad_add_fusion.ids, s32[16]{0:T(128)S(1)} %reshape.58.slots, f32[1024,256]{1,0:T(8,128)S(1)} %copy-done, f32[16,128,256]{2,1,0:T(8,128)} %bitcast.5.kids_ref, f32[16,224,128]{2,1,0:T(8,128)} %all-to-all-done.2.own_ref, f32[16,224,128]{2,1,0:T(8,128)} %collective-permute-done.other_ref, ...), custom_call_target="tpu_custom_call" | custom-call | flops 6000000000 | bytes 20971520 | tf_op jit(solution)/shard_map/tail/pallas_call | solution.py:235
  (7 shorter events, 0.1 us)
Async XLA Ops:
  0.0 24.9 %slice-start = ((f32[1024,256]{1,0:T(8,128)}), f32[1024,128]{1,0:T(8,128)S(1)}, s32[]{:S(2)}) async-start(f32[1024,256]{1,0:T(8,128)} %front_ref.1), calls=%async_computation.8 | async-start | bytes 1048576 | tf_op jit(solution)/shard_map/slice | solution.py:277
  16.4 17.5 %all-to-all-start.6 = ((f32[8,32,128]{2,1,0:T(8,128)}), f32[8,32,128]{2,1,0:T(8,128)S(1)}, u32[]{:S(2)}, u32[]{:S(2)}) async-start(f32[8,32,128]{2,1,0:T(8,128)} %broadcast_in_dim.42), calls=%async_computation.6 | async-start | bytes 262144 | tf_op jit(solution)/shard_map/all_to_all | solution.py:248
  51.0 31.8 %all-to-all-start.7 = ((f32[16,256,128]{2,1,0:T(8,128)}), f32[16,256,128]{2,1,0:T(8,128)S(1)}, u32[]{:S(2)}, u32[]{:S(2)}) async-start(f32[16,256,128]{2,1,0:T(8,128)} %broadcast_in_dim.44), calls=%async_computation.7 | async-start | bytes 4194304 | tf_op jit(solution)/shard_map/all_to_all | solution.py:248
  84.3 31.7 %all-to-all-start.2 = ((f32[16,224,128]{2,1,0:T(8,128)}), f32[16,224,128]{2,1,0:T(8,128)}, u32[]{:S(2)}, u32[]{:S(2)}) async-start(f32[16,224,128]{2,1,0:T(8,128)} %broadcast_in_dim.38), calls=%async_computation.2 | async-start | bytes 3670016 | tf_op jit(solution)/shard_map/all_to_all | solution.py:248
  117.1 30.3 %all-to-all-start.3 = ((f32[8,8,32,128]{3,2,1,0:T(8,128)}), f32[8,8,32,128]{3,2,1,0:T(8,128)S(1)}, u32[]{:S(2)}, u32[]{:S(2)}) async-start(f32[8,8,32,128]{3,2,1,0:T(8,128)} %broadcast_in_dim.39), calls=%async_computation.3 | async-start | bytes 2097152 | tf_op jit(solution)/shard_map/all_to_all | solution.py:248
  120.7 66.4 %collective-permute-start.1 = (f32[16,256,128]{2,1,0:T(8,128)S(1)}, f32[16,256,128]{2,1,0:T(8,128)}, u32[]{:S(2)}, u32[]{:S(2)}) collective-permute-start(f32[16,256,128]{2,1,0:T(8,128)S(1)} %all-to-all-done.7.own_ref), channel_id=1, source_target_pairs={{0,64},{64,0},{1,65},{65,1},{2,66},{66,2},{3,67},{67,3},{4,68},{68... | collective-permute-start | bytes 6291464 | tf_op jit(solution)/shard_map/ppermute | solution.py:252
  147.5 31.7 %all-to-all-start = ((f32[2,256,4,256]{3,1,0,2:T(8,128)}), f32[2,256,4,256]{3,1,0,2:T(8,128)}, u32[]{:S(2)}, u32[]{:S(2)}) async-start(f32[2,256,4,256]{3,1,0,2:T(8,128)} %bitcast.74), calls=%async_computation | async-start | bytes 4194304 | tf_op jit(solution)/shard_map/all_to_all | solution.py:294
  152.0 82.2 %collective-permute-start = (f32[16,224,128]{2,1,0:T(8,128)}, f32[16,224,128]{2,1,0:T(8,128)}, u32[]{:S(2)}, u32[]{:S(2)}) collective-permute-start(f32[16,224,128]{2,1,0:T(8,128)} %all-to-all-done.2.own_ref), channel_id=1, source_target_pairs={{0,64},{64,0},{1,65},{65,1},{2,66},{66,2},{3,67},{67,3},{4,68},{68... | collective-permute-start | bytes 5505032 | tf_op jit(solution)/shard_map/ppermute | solution.py:252
  179.2 55.0 %all-to-all-start.4 = ((f32[32,64,128]{2,1,0:T(8,128)}), f32[32,64,128]{2,1,0:T(8,128)S(1)}, u32[]{:S(2)}, u32[]{:S(2)}) async-start(f32[32,64,128]{2,1,0:T(8,128)} %bitcast.76), calls=%async_computation.4 | async-start | bytes 2097152 | tf_op jit(solution)/shard_map/all_to_all | solution.py:291
  231.5 1.3 copy-start.1
  232.8 1.4 copy-start.3
  234.2 1.2 copy-start
  235.4 1.6 copy-start.2
  237.0 1.6 copy-start.4
